TPU v7x, 128 devices: a whole 4x4x4 slice. The times are simulated.
128 devices in a mesh: inner: 8 (over z, y_hi), outer: 16 (over x, y_lo, core).
Axes of the slice: x: 4, y: 4 (y_hi: 2, y_lo: 2; y = y_hi * 2 + y_lo), z: 4, core: 2. Of those that a mesh axis runs over, the one named last changes fastest.
Arguments:
- query: float32 [16384, 4096], P(('inner', 'outer')), may hold values from -14 to 14
- keys: float32 [16384, 1024], P(('inner', 'outer')), may hold values from -4.5 to 4.5
- values: float32 [16384, 1024], P(('inner', 'outer')), may hold values from -6 to 6
- grad_out: float32 [16384, 4096], P(('inner', 'outer')), may hold values from -6 to 6
- segment_number: int32 [128, 2], replicated, may hold values from 0 to 255, as said below
Outputs:
- asker_derivative: float32 [16384, 4096], P(('inner', 'outer'))
- grad_keys: float32 [16384, 1024], P(('inner', 'outer'))
- grad_values: float32 [16384, 1024], P(('inner', 'outer'))
Inputs may be any that keep to these rules, and one draw needn't show every extreme that they name: `segment_number`: row d holds stretches c and 255 - c with c < 128; every stretch of the sequence appears once.
All inputs are finite; a program needn't handle non-finite values.
Results may differ from a plain program's by a relative error of at most 0.002.
Values sent between devices are 32-bit elements; how exact they have to be, the bound alone decides.
No kernel may reach another device: no remote copies, remote signals or barrier semaphores. Data moves between devices by JAX's collectives and lax.ppermute only.
A program may use at most 128 MiB of HBM per device.

v0:
```python
import jax
import jax.numpy as jnp
from jax import lax
from jax.sharding import PartitionSpec as P

ASKER_PLANES = 32
KEY_VALUE_HEADS = 8
HEAD_SIZE = 128


def from_behind(x, axis, by):
    size = lax.axis_size(axis)
    return lax.ppermute(x, axis, [(i, (i + by) % size) for i in range(size)])


def token_positions(stretch_rows, row_count):
    half_rows = row_count // 2
    local_rows = jnp.arange(row_count, dtype=jnp.int32)
    return stretch_rows[:, local_rows // half_rows] * half_rows + local_rows % half_rows


def local(query, keys, values, grad_out, segment_number):
    inner_count = lax.axis_size("inner")
    outer_count = lax.axis_size("outer")
    inner_index = lax.axis_index("inner")
    outer_index = lax.axis_index("outer")
    row_count = query.shape[0]
    group_list = ASKER_PLANES // KEY_VALUE_HEADS
    head_width = group_list * HEAD_SIZE
    score_scale = HEAD_SIZE ** (-0.5)
    cycle_base = jnp.arange(inner_count, dtype=jnp.int32) * outer_count
    own_stretches = segment_number[cycle_base + outer_index]
    prev_stretches = segment_number[cycle_base + (outer_index - 1) % outer_count]
    key_positions = token_positions(
        jnp.concatenate([own_stretches, prev_stretches], 0), row_count
    ).reshape(-1)
    query_positions = token_positions(
        segment_number[inner_index * outer_count + outer_index][None], row_count
    )[0]
    own_keys, own_values = (
        lax.all_gather(keys, "inner", axis=0, tiled=True),
        lax.all_gather(values, "inner", axis=0, tiled=True),
    )
    prev_keys, prev_values = from_behind((own_keys, own_values), "outer", 1)
    adjacent_keys = jnp.concatenate([own_keys, prev_keys], 0)
    adjacent_values = jnp.concatenate([own_values, prev_values], 0)
    key_total = adjacent_keys.shape[0]
    visible = key_positions[None, :] <= query_positions[:, None]

    def head_stride(head_index, running):
        query_grads, key_grads, value_grads = running
        query_head = lax.dynamic_slice_in_dim(
            query, head_index * head_width, head_width, 1
        ).reshape(row_count, group_list, HEAD_SIZE)
        out_head = lax.dynamic_slice_in_dim(
            grad_out, head_index * head_width, head_width, 1
        ).reshape(row_count, group_list, HEAD_SIZE)
        keys_head = lax.dynamic_slice_in_dim(adjacent_keys, head_index * HEAD_SIZE, HEAD_SIZE, 1)
        values_head = lax.dynamic_slice_in_dim(
            adjacent_values, head_index * HEAD_SIZE, HEAD_SIZE, 1
        )
        scores = (
            jnp.einsum("tgd,ld->gtl", query_head, keys_head, precision=lax.Precision.HIGHEST)
            * score_scale
        )
        scores = jnp.where(visible[None], scores, -jnp.inf)
        row_peak = jnp.max(scores, axis=-1, keepdims=True)
        shifted_exp = jnp.exp(scores - row_peak)
        weights = shifted_exp / jnp.sum(shifted_exp, axis=-1, keepdims=True)
        weight_grads = jnp.einsum(
            "tgd,ld->gtl", out_head, values_head, precision=lax.Precision.HIGHEST
        )
        row_delta = jnp.sum(weights * weight_grads, axis=-1, keepdims=True)
        score_grads = weights * (weight_grads - row_delta) * score_scale
        query_grad = jnp.einsum(
            "gtl,ld->tgd", score_grads, keys_head, precision=lax.Precision.HIGHEST
        ).reshape(row_count, head_width)
        key_grad = jnp.einsum(
            "gtl,tgd->ld", score_grads, query_head, precision=lax.Precision.HIGHEST
        )
        value_grad = jnp.einsum("gtl,tgd->ld", weights, out_head, precision=lax.Precision.HIGHEST)
        query_grads = lax.dynamic_update_slice_in_dim(
            query_grads, query_grad, head_index * head_width, 1
        )
        key_grads = lax.dynamic_update_slice_in_dim(key_grads, key_grad, head_index * HEAD_SIZE, 1)
        value_grads = lax.dynamic_update_slice_in_dim(
            value_grads, value_grad, head_index * HEAD_SIZE, 1
        )
        return (query_grads, key_grads, value_grads)

    initial_state = (
        jnp.zeros((row_count, ASKER_PLANES * HEAD_SIZE), jnp.float32),
        jnp.zeros((key_total, KEY_VALUE_HEADS * HEAD_SIZE), jnp.float32),
        jnp.zeros((key_total, KEY_VALUE_HEADS * HEAD_SIZE), jnp.float32),
    )
    asker_derivative, lookup_partial_contributions, payload_partial_contributions = lax.fori_loop(
        0, KEY_VALUE_HEADS, head_stride, initial_state
    )
    local_interval = inner_count * row_count
    returning_lookup_vectors, returning_payload_vectors = from_behind(
        (
            lookup_partial_contributions[local_interval:],
            payload_partial_contributions[local_interval:],
        ),
        "outer",
        -1,
    )
    grad_keys, grad_values = (
        lax.psum_scatter(
            lookup_partial_contributions[:local_interval] + returning_lookup_vectors,
            "inner",
            scatter_dimension=0,
            tiled=True,
        ),
        lax.psum_scatter(
            payload_partial_contributions[:local_interval] + returning_payload_vectors,
            "inner",
            scatter_dimension=0,
            tiled=True,
        ),
    )
    return (asker_derivative, grad_keys, grad_values)


def solution(mesh):
    return jax.shard_map(
        local,
        mesh=mesh,
        in_specs=(
            P(("inner", "outer"), None),
            P(("inner", "outer"), None),
            P(("inner", "outer"), None),
            P(("inner", "outer"), None),
            P(),
        ),
        out_specs=(
            P(("inner", "outer"), None),
            P(("inner", "outer"), None),
            P(("inner", "outer"), None),
        ),
        check_vma=False,
    )
```

profile of v0, /device:TPU:1, one launch (start us, length us, event | category | flops | bytes accessed | tf_op | source)
XLA Modules:
  0.0 786.7 jit_solution(1432042297379179411)
XLA Ops:
  8.7 76.1 %all-gather.5.cloned.1.call-done = f32[1024,1024]{1,0:T(8,128)} async-done(((f32[128,1024]{1,0:T(8,128)}), f32[1024,1024]{1,0:T(8,128)}) %all-gather.5.cloned.1.call-update) | async-done | bytes 4194320 | tf_op jit(solution)/shard_map/all_gather | solution.py:42
  86.0 105.1 %all-gather.3.cloned.1.call-done = f32[1024,1024]{1,0:T(8,128)} async-done(((f32[128,1024]{1,0:T(8,128)}), f32[1024,1024]{1,0:T(8,128)}) %all-gather.3.cloned.1.call-update) | async-done | bytes 4194320 | tf_op jit(solution)/shard_map/all_gather | solution.py:41
  198.0 8.5 %pad_maximum_fusion.1 = f32[2048,1024]{1,0:T(8,128)} fusion(f32[1024,1024]{1,0:T(8,128)} %collective-permute-done.1, f32[1024,1024]{1,0:T(8,128)} %all-gather.5.cloned.1.call-done), kind=kLoop, calls=%fused_computation.35 | loop fusion | flops 2097152 | bytes 16777216 | tf_op jit(solution)/shard_map/concatenate | solution.py:46
  206.5 31.7 %collective-permute-done = f32[1024,1024]{1,0:T(8,128)} collective-permute-done((f32[1024,1024]{1,0:T(8,128)}, f32[1024,1024]{1,0:T(8,128)}, u32[]{:S(2)}, u32[]{:S(2)}) %collective-permute-start) | collective-permute-done | bytes 4194336 | tf_op jit(solution)/shard_map/ppermute | solution.py:13
  238.2 6.8 pad_maximum_fusion
  253.8 258.6 %while.18 = (s32[]{:T(128)}, f32[128,4096]{1,0:T(8,128)S(1)}, f32[2048,1024]{1,0:T(8,128)}, f32[2048,1024]{1,0:T(8,128)}, f32[2048,1024]{1,0:T(8,128)}, /*index=...) while((s32[]{:T(128)}, f32[128,4096]{1,0:T(8,128)S(1)}, ...), condition=%wide.region_4.5_spmd.clone, body=%wide.region_0.4_spmd.clone.sunk | while | flops 8075344384 | bytes 98341736 | solution.py:96
  255.4 5.0 fusion.60
  261.0 6.3 fusion.62
  267.3 5.7 fusion.63
  273.2 8.1 %fusion.64 = f32[2048,1024]{1,0:T(8,128)} fusion(f32[2048,1024]{1,0:T(8,128)} %get-tuple-element.334, s32[]{:T(128)S(6)} %select_n.139, f32[128,4,128]{0,2,1:T(8,128)S(1)} %bitcast.87, f32[2048,128,4]{1,0,2:T(8,128)} %copy-done.5, f32[4,128]{1,0:T(4,128)S(1)} %get-tuple-element.315, f32[4,128,2048]{1,2,0:T(8,128)} %copy-done, ...), kind=kOutput, calls=%fused_computation.16.clone.1 | convolution fusion | flops 1615855616 | bytes 9705476 | tf_op jit(solution)/shard_map/while/body/eval_jaxpr/gtl,tgd->ld/dot_general | solution.py:78
  281.3 4.7 fusion.65
  287.8 5.0 fusion.60
  293.3 6.3 fusion.62
  299.6 5.7 fusion.63
  305.5 8.1 %fusion.64 = f32[2048,1024]{1,0:T(8,128)} fusion(f32[2048,1024]{1,0:T(8,128)} %get-tuple-element.334, s32[]{:T(128)S(6)} %select_n.139, f32[128,4,128]{0,2,1:T(8,128)S(1)} %bitcast.87, f32[2048,128,4]{1,0,2:T(8,128)} %copy-done.5, f32[4,128]{1,0:T(4,128)S(1)} %get-tuple-element.315, f32[4,128,2048]{1,2,0:T(8,128)} %copy-done, ...), kind=kOutput, calls=%fused_computation.16.clone.1 | convolution fusion | flops 1615855616 | bytes 9705476 | tf_op jit(solution)/shard_map/while/body/eval_jaxpr/gtl,tgd->ld/dot_general | solution.py:78
  320.1 5.0 fusion.60
  325.6 6.3 fusion.62
  331.9 5.7 fusion.63
  337.8 8.1 %fusion.64 = f32[2048,1024]{1,0:T(8,128)} fusion(f32[2048,1024]{1,0:T(8,128)} %get-tuple-element.334, s32[]{:T(128)S(6)} %select_n.139, f32[128,4,128]{0,2,1:T(8,128)S(1)} %bitcast.87, f32[2048,128,4]{1,0,2:T(8,128)} %copy-done.5, f32[4,128]{1,0:T(4,128)S(1)} %get-tuple-element.315, f32[4,128,2048]{1,2,0:T(8,128)} %copy-done, ...), kind=kOutput, calls=%fused_computation.16.clone.1 | convolution fusion | flops 1615855616 | bytes 9705476 | tf_op jit(solution)/shard_map/while/body/eval_jaxpr/gtl,tgd->ld/dot_general | solution.py:78
  345.9 4.8 fusion.65
  352.4 5.0 fusion.60
  358.0 6.3 fusion.62
  364.3 5.7 fusion.63
  370.2 8.1 %fusion.64 = f32[2048,1024]{1,0:T(8,128)} fusion(f32[2048,1024]{1,0:T(8,128)} %get-tuple-element.334, s32[]{:T(128)S(6)} %select_n.139, f32[128,4,128]{0,2,1:T(8,128)S(1)} %bitcast.87, f32[2048,128,4]{1,0,2:T(8,128)} %copy-done.5, f32[4,128]{1,0:T(4,128)S(1)} %get-tuple-element.315, f32[4,128,2048]{1,2,0:T(8,128)} %copy-done, ...), kind=kOutput, calls=%fused_computation.16.clone.1 | convolution fusion | flops 1615855616 | bytes 9705476 | tf_op jit(solution)/shard_map/while/body/eval_jaxpr/gtl,tgd->ld/dot_general | solution.py:78
  378.3 4.8 fusion.65
  384.7 5.0 fusion.60
  390.3 6.3 fusion.62
  396.6 5.7 fusion.63
  402.5 8.1 %fusion.64 = f32[2048,1024]{1,0:T(8,128)} fusion(f32[2048,1024]{1,0:T(8,128)} %get-tuple-element.334, s32[]{:T(128)S(6)} %select_n.139, f32[128,4,128]{0,2,1:T(8,128)S(1)} %bitcast.87, f32[2048,128,4]{1,0,2:T(8,128)} %copy-done.5, f32[4,128]{1,0:T(4,128)S(1)} %get-tuple-element.315, f32[4,128,2048]{1,2,0:T(8,128)} %copy-done, ...), kind=kOutput, calls=%fused_computation.16.clone.1 | convolution fusion | flops 1615855616 | bytes 9705476 | tf_op jit(solution)/shard_map/while/body/eval_jaxpr/gtl,tgd->ld/dot_general | solution.py:78
  417.0 5.0 fusion.60
  422.6 6.3 fusion.62
  428.9 5.7 fusion.63
  434.8 8.1 %fusion.64 = f32[2048,1024]{1,0:T(8,128)} fusion(f32[2048,1024]{1,0:T(8,128)} %get-tuple-element.334, s32[]{:T(128)S(6)} %select_n.139, f32[128,4,128]{0,2,1:T(8,128)S(1)} %bitcast.87, f32[2048,128,4]{1,0,2:T(8,128)} %copy-done.5, f32[4,128]{1,0:T(4,128)S(1)} %get-tuple-element.315, f32[4,128,2048]{1,2,0:T(8,128)} %copy-done, ...), kind=kOutput, calls=%fused_computation.16.clone.1 | convolution fusion | flops 1615855616 | bytes 9705476 | tf_op jit(solution)/shard_map/while/body/eval_jaxpr/gtl,tgd->ld/dot_general | solution.py:78
  442.9 4.8 fusion.65
  449.4 5.0 fusion.60
  454.9 6.3 fusion.62
  461.2 5.7 fusion.63
  467.1 8.1 %fusion.64 = f32[2048,1024]{1,0:T(8,128)} fusion(f32[2048,1024]{1,0:T(8,128)} %get-tuple-element.334, s32[]{:T(128)S(6)} %select_n.139, f32[128,4,128]{0,2,1:T(8,128)S(1)} %bitcast.87, f32[2048,128,4]{1,0,2:T(8,128)} %copy-done.5, f32[4,128]{1,0:T(4,128)S(1)} %get-tuple-element.315, f32[4,128,2048]{1,2,0:T(8,128)} %copy-done, ...), kind=kOutput, calls=%fused_computation.16.clone.1 | convolution fusion | flops 1615855616 | bytes 9705476 | tf_op jit(solution)/shard_map/while/body/eval_jaxpr/gtl,tgd->ld/dot_general | solution.py:78
  475.2 4.8 fusion.65
  481.7 5.0 fusion.60
  487.3 6.3 fusion.62
  493.5 5.7 fusion.63
  499.5 8.1 %fusion.64 = f32[2048,1024]{1,0:T(8,128)} fusion(f32[2048,1024]{1,0:T(8,128)} %get-tuple-element.334, s32[]{:T(128)S(6)} %select_n.139, f32[128,4,128]{0,2,1:T(8,128)S(1)} %bitcast.87, f32[2048,128,4]{1,0,2:T(8,128)} %copy-done.5, f32[4,128]{1,0:T(4,128)S(1)} %get-tuple-element.315, f32[4,128,2048]{1,2,0:T(8,128)} %copy-done, ...), kind=kOutput, calls=%fused_computation.16.clone.1 | convolution fusion | flops 1615855616 | bytes 9705476 | tf_op jit(solution)/shard_map/while/body/eval_jaxpr/gtl,tgd->ld/dot_general | solution.py:78
  520.1 44.3 %collective-permute-done.2 = f32[1024,1024]{1,0:T(8,128)S(1)} collective-permute-done((f32[1024,1024]{1,0:T(8,128)S(1)}, f32[1024,1024]{1,0:T(8,128)S(1)}, u32[]{:S(2)}, u32[]{:S(2)}) %collective-permute-start.2) | collective-permute-done | bytes 4194336 | tf_op jit(solution)/shard_map/ppermute | solution.py:13
  571.7 69.0 %collective-permute-done.3 = f32[1024,1024]{1,0:T(8,128)S(1)} collective-permute-done((f32[1024,1024]{1,0:T(8,128)S(1)}, f32[1024,1024]{1,0:T(8,128)S(1)}, u32[]{:S(2)}, u32[]{:S(2)}) %collective-permute-start.3) | collective-permute-done | bytes 4194336 | tf_op jit(solution)/shard_map/ppermute | solution.py:13
  640.7 5.2 slice_add_fusion
  645.9 46.0 %reduce-scatter.3.cloned.1.call-done = f32[128,1024]{1,0:T(8,128)} async-done(((f32[1024,1024]{1,0:T(8,128)}), f32[128,1024]{1,0:T(8,128)}) %reduce-scatter.3.cloned.1.call-update) | async-done | bytes 524304 | tf_op jit(solution)/shard_map/reduce_scatter | solution.py:109
  691.9 88.2 %reduce-scatter.5.cloned.1.call-done = f32[128,1024]{1,0:T(8,128)} async-done(((f32[1024,1024]{1,0:T(8,128)}), f32[128,1024]{1,0:T(8,128)}) %reduce-scatter.5.cloned.1.call-update) | async-done | bytes 524304 | tf_op jit(solution)/shard_map/reduce_scatter | solution.py:115
  (151 shorter events, 66.7 us)
Async XLA Ops:
  7.2 77.6 %all-gather.5.cloned.1.call-start = ((), (), s32[]{:S(2)}) async-start(), calls=%async_computation.3 | async-start | bytes 4718592 | tf_op jit(solution)/shard_map/all_gather | solution.py:42
  7.9 183.2 %all-gather.3.cloned.1.call-start = ((), (), s32[]{:S(2)}) async-start(), calls=%async_computation.2 | async-start | bytes 4718592 | tf_op jit(solution)/shard_map/all_gather | solution.py:41
  8.6 683.3 %reduce-scatter.3.cloned.1.call-start = ((), (), s32[]{:S(2)}) async-start(), calls=%async_computation.4 | async-start | bytes 4718592 | tf_op jit(solution)/shard_map/reduce_scatter | solution.py:109
  84.8 113.3 %collective-permute-start.1 = (f32[1024,1024]{1,0:T(8,128)}, f32[1024,1024]{1,0:T(8,128)}, u32[]{:S(2)}, u32[]{:S(2)}) collective-permute-start(f32[1024,1024]{1,0:T(8,128)} %all-gather.5.cloned.1.call-done), channel_id=1, source_target_pairs={{0,1},{1,2},{2,3},{3,4},{4,5},{5,6},{6,7},{7,8},{8,9},{9,10},{10,1... | collective-permute-start | bytes 12582920 | tf_op jit(solution)/shard_map/ppermute | solution.py:13
  191.1 47.0 %collective-permute-start = (f32[1024,1024]{1,0:T(8,128)}, f32[1024,1024]{1,0:T(8,128)}, u32[]{:S(2)}, u32[]{:S(2)}) collective-permute-start(f32[1024,1024]{1,0:T(8,128)} %all-gather.3.cloned.1.call-done), channel_id=1, source_target_pairs={{0,1},{1,2},{2,3},{3,4},{4,5},{5,6},{6,7},{7,8},{8,9},{9,10},{10,1... | collective-permute-start | bytes 12582920 | tf_op jit(solution)/shard_map/ppermute | solution.py:13
  198.0 40.2 %copy-start.3 = (f32[1024,1024]{1,0:T(8,128)S(1)}, f32[1024,1024]{1,0:T(8,128)}, u32[]{:S(2)}) copy-start(f32[1024,1024]{1,0:T(8,128)} %all-gather.3.cloned.1.call-done) | copy-start | bytes 12582916
  260.4 6.9 copy-start
  267.3 5.7 copy-start.5
  273.2 8.1 %copy-start.1 = (f32[4,128,2048]{1,2,0:T(8,128)S(1)}, f32[4,128,2048]{1,2,0:T(8,128)}, u32[]{:S(2)}) copy-start(f32[4,128,2048]{1,2,0:T(8,128)} %copy-done) | copy-start | bytes 12582916 | tf_op jit(solution)/shard_map/while
  292.8 6.9 copy-start
  299.6 5.7 copy-start.5
  305.5 8.1 %copy-start.1 = (f32[4,128,2048]{1,2,0:T(8,128)S(1)}, f32[4,128,2048]{1,2,0:T(8,128)}, u32[]{:S(2)}) copy-start(f32[4,128,2048]{1,2,0:T(8,128)} %copy-done) | copy-start | bytes 12582916 | tf_op jit(solution)/shard_map/while
  325.0 6.9 copy-start
  331.9 5.7 copy-start.5
  337.8 8.1 %copy-start.1 = (f32[4,128,2048]{1,2,0:T(8,128)S(1)}, f32[4,128,2048]{1,2,0:T(8,128)}, u32[]{:S(2)}) copy-start(f32[4,128,2048]{1,2,0:T(8,128)} %copy-done) | copy-start | bytes 12582916 | tf_op jit(solution)/shard_map/while
  357.4 6.9 copy-start
  364.2 5.7 copy-start.5
  370.2 8.1 %copy-start.1 = (f32[4,128,2048]{1,2,0:T(8,128)S(1)}, f32[4,128,2048]{1,2,0:T(8,128)}, u32[]{:S(2)}) copy-start(f32[4,128,2048]{1,2,0:T(8,128)} %copy-done) | copy-start | bytes 12582916 | tf_op jit(solution)/shard_map/while
  389.7 6.9 copy-start
  396.6 5.7 copy-start.5
  402.5 8.1 %copy-start.1 = (f32[4,128,2048]{1,2,0:T(8,128)S(1)}, f32[4,128,2048]{1,2,0:T(8,128)}, u32[]{:S(2)}) copy-start(f32[4,128,2048]{1,2,0:T(8,128)} %copy-done) | copy-start | bytes 12582916 | tf_op jit(solution)/shard_map/while
  422.0 6.9 copy-start
  428.9 5.7 copy-start.5
  434.8 8.1 %copy-start.1 = (f32[4,128,2048]{1,2,0:T(8,128)S(1)}, f32[4,128,2048]{1,2,0:T(8,128)}, u32[]{:S(2)}) copy-start(f32[4,128,2048]{1,2,0:T(8,128)} %copy-done) | copy-start | bytes 12582916 | tf_op jit(solution)/shard_map/while
  454.4 6.9 copy-start
  461.2 5.7 copy-start.5
  467.1 8.1 %copy-start.1 = (f32[4,128,2048]{1,2,0:T(8,128)S(1)}, f32[4,128,2048]{1,2,0:T(8,128)}, u32[]{:S(2)}) copy-start(f32[4,128,2048]{1,2,0:T(8,128)} %copy-done) | copy-start | bytes 12582916 | tf_op jit(solution)/shard_map/while
  486.7 6.9 copy-start
  493.5 5.7 copy-start.5
  499.4 8.2 %copy-start.1 = (f32[4,128,2048]{1,2,0:T(8,128)S(1)}, f32[4,128,2048]{1,2,0:T(8,128)}, u32[]{:S(2)}) copy-start(f32[4,128,2048]{1,2,0:T(8,128)} %copy-done) | copy-start | bytes 12582916 | tf_op jit(solution)/shard_map/while
  512.3 3.3 copy-start.4
  512.3 52.1 %copy-start.2 = (f32[2048,1024]{1,0:T(8,128)S(1)}, f32[2048,1024]{1,0:T(8,128)}, u32[]{:S(2)}) copy-start(f32[2048,1024]{1,0:T(8,128)} %get-tuple-element.160) | copy-start | bytes 25165828
  515.7 48.7 %collective-permute-start.2 = (f32[1024,1024]{1,0:T(8,128)S(1)}, f32[1024,1024]{1,0:T(8,128)S(1)}, u32[]{:S(2)}, u32[]{:S(2)}) collective-permute-start(f32[1024,1024]{1,0:T(8,128)S(1)} %slice.13), channel_id=1, source_target_pairs={{0,15},{1,0},{2,1},{3,2},{4,3},{5,4},{6,5},{7,6},{8,7},{9,8},{10,9... | collective-permute-start | bytes 12582920 | tf_op jit(solution)/shard_map/ppermute | solution.py:13
  567.3 212.8 %reduce-scatter.5.cloned.1.call-start = ((), (), s32[]{:S(2)}) async-start(), calls=%async_computation.5 | async-start | bytes 4718592 | tf_op jit(solution)/shard_map/reduce_scatter | solution.py:115
  569.9 70.9 %collective-permute-start.3 = (f32[1024,1024]{1,0:T(8,128)S(1)}, f32[1024,1024]{1,0:T(8,128)S(1)}, u32[]{:S(2)}, u32[]{:S(2)}) collective-permute-start(f32[1024,1024]{1,0:T(8,128)S(1)} %slice.15), channel_id=1, source_target_pairs={{0,15},{1,0},{2,1},{3,2},{4,3},{5,4},{6,5},{7,6},{8,7},{9,8},{10,9... | collective-permute-start | bytes 12582920 | tf_op jit(solution)/shard_map/ppermute | solution.py:13
Sparse Core Ops, SparseCore 0:
  10.3 74.3 all-gather.4
  87.1 103.9 all-gather.2
  567.4 124.4 reduce-scatter.2
  696.7 83.4 reduce-scatter.4
where the time goes:
time: 788 us; the launch traced here: 787 us
  waiting for transfers between devices  462 us (59%)
  matrix products  239 us (30%)
  other arithmetic  32.1 us (4%)
  local copies, waits for them, and re-layouts  30.5 us (4%)
  between operations  13.9 us (2%)
  starting transfers between devices  8.99 us (1%)
    ppermute x4, waiting for transfers between devices, from_behind(): return lax.ppermute(x, axis, [(i, (i + by) % size) for i in range(size)])  145 us
    all_gather x1, waiting for transfers between devices, local(): lax.all_gather(keys, 'inner', axis=0, tiled=True)  105 us
    reduce_scatter x1, waiting for transfers between devices, local(): lax.psum_scatter(payload_partial_contributions[:local_interval] + returni...  88.2 us
    all_gather x1, waiting for transfers between devices, local(): lax.all_gather(values, 'inner', axis=0, tiled=True)  76.1 us
    dot_general x8, matrix products, head_stride(): jnp.einsum('gtl,tgd->ld', score_grads, query_head, precision=lax.Precisio...  64.9 us
    dot_general x8, matrix products, head_stride(): jnp.einsum('tgd,ld->gtl', out_head, values_head, precision=lax.Precision....  50 us
    reduce_scatter x1, waiting for transfers between devices, local(): lax.psum_scatter(lookup_partial_contributions[:local_interval] + returnin...  46 us
    dot_general x8, matrix products, head_stride(): jnp.einsum('gtl,ld->tgd', score_grads, keys_head, precision=lax.Precision...  45.7 us
  transfers between devices with their start and end apart: 8, of which 7 were waited for; matrix products, arithmetic and copies ran while one was open for 3% of the time, Pallas kernels for 0%

commit v1 on v0

v1 whole, which is shorter than its diff:
```python
import functools
import math

import jax
import jax.numpy as jnp
from jax import lax
from jax.experimental import pallas as pl
from jax.experimental.pallas import tpu as pltpu
from jax.sharding import PartitionSpec as P

ASKER_PLANES = 32
KEY_VALUE_HEADS = 8
HEAD_SIZE = 128
GROUP_LIST = ASKER_PLANES // KEY_VALUE_HEADS
HEAD_WIDTH = GROUP_LIST * HEAD_SIZE
TILE = 256
SCORE_SCALE = HEAD_SIZE ** (-0.5)
LOG2E = math.log2(math.e)
F32 = jnp.float32
BF16 = jnp.bfloat16


def split2(x):
    high = x.astype(BF16)
    return high, (x - high.astype(F32)).astype(BF16)


def split3(x):
    high = x.astype(BF16)
    rest = x - high.astype(F32)
    middle = rest.astype(BF16)
    return high, middle, (rest - middle.astype(F32)).astype(BF16)


def dot(a, b):
    return jnp.dot(a, b, preferred_element_type=F32)


def fold(x, op):
    return op(x.reshape(x.shape[0] // 8, 8, x.shape[1]), axis=0)


def attention_kernel(
    inner_count, outer_count,
    seg, q_ref, do_ref, own_ref, prev_ref,
    dq_ref, down_ref, dprev_ref,
    rank, low_half, ksort, kcat, vcat, ktrans, dk_acc, dv_acc,
    s_scr, dp_scr,
):
    step = pl.program_id(0)
    blocks = 2 * inner_count
    stretch = own_ref.shape[1] // 2

    @pl.when(step == 0)
    def _():
        outer = lax.axis_index("outer")
        before = lax.rem(outer + outer_count - 1, outer_count)
        first, second = [], []
        for j in range(blocks):
            device = (j % inner_count) * outer_count + (outer if j < inner_count else before)
            first.append(seg[0, device])
            second.append(seg[1, device])
        lows = [jnp.minimum(a, b) for a, b in zip(first, second)]
        for j in range(blocks):
            below = jnp.int32(0)
            for other in range(blocks):
                if other != j:
                    below = below + (lows[other] < lows[j]).astype(jnp.int32)
            rank[j] = below
            low_half[j] = (second[j] < first[j]).astype(jnp.int32)
        for j in range(blocks):
            ref, at = (own_ref, j) if j < inner_count else (prev_ref, j - inner_count)
            for half in range(2):
                slot = jnp.where(low_half[j] == half, rank[j], 2 * blocks - 1 - rank[j])
                to = pl.ds(pl.multiple_of(slot * stretch, stretch), stretch)
                both = ref[at, half * stretch : (half + 1) * stretch, :]
                key, value = both[:, :HEAD_SIZE], both[:, HEAD_SIZE:]
                ksort[to, :] = key
                h, m, l = split3(key)
                kcat[to, :] = jnp.concatenate([h, h, m, h, l, m], axis=1)
                h, l = split2(value)
                vcat[to, :] = jnp.concatenate([h, h, l, l], axis=1)
        for t in range(ksort.shape[0] // TILE):
            h, l = split2(ksort[t * TILE : (t + 1) * TILE, :].T)
            ktrans[t] = jnp.concatenate([h, l], axis=0)
        dk_acc[...] = jnp.zeros_like(dk_acc)
        dv_acc[...] = jnp.zeros_like(dv_acc)

    place = rank[step]
    low = low_half[step]
    per_tile = TILE // stretch
    for kind in range(2):
        offset = pl.multiple_of(jnp.where(low == kind, 0, stretch), stretch)
        reach = place if kind == 0 else 2 * blocks - 1 - place
        last = reach // per_tile
        rows = pl.ds(offset, stretch)
        q = jnp.concatenate(
            [q_ref[0, rows, g * HEAD_SIZE : (g + 1) * HEAD_SIZE] for g in range(GROUP_LIST)], axis=0
        ) * (SCORE_SCALE * LOG2E)
        do = jnp.concatenate(
            [do_ref[0, rows, g * HEAD_SIZE : (g + 1) * HEAD_SIZE] for g in range(GROUP_LIST)], axis=0
        )
        h, m, l = split3(q.T)
        qt = jnp.concatenate([h, m, h, l, h, m], axis=0)
        h, l = split2(q)
        q_pair = jnp.concatenate([h, l], axis=1)
        q_rhs = jnp.concatenate([q_pair, q_pair], axis=0)
        h, l = split2(do.T)
        dot_t = jnp.concatenate([h, l, h, l], axis=0)
        h, l = split2(do)
        do_pair = jnp.concatenate([h, l], axis=1)
        do_rhs = jnp.concatenate([do_pair, do_pair], axis=0)

        def scores(t):
            at = pl.ds(pl.multiple_of(t * TILE, TILE), TILE)
            return at, dot(kcat[at, :], qt), dot(vcat[at, :], dot_t)

        def open_tile(t, peak):
            at, s, dp = scores(t)
            s_scr[at, :] = s
            dp_scr[at, :] = dp
            return jnp.maximum(peak, fold(s, jnp.max))

        peak = lax.fori_loop(0, last, open_tile, jnp.full((8, TILE), -jnp.inf, F32))
        at, s, dp = scores(last)
        key_at = last * TILE + lax.broadcasted_iota(jnp.int32, (TILE, TILE), 0)
        token = lax.rem(lax.broadcasted_iota(jnp.int32, (TILE, TILE), 1), stretch)
        s = jnp.where(key_at <= reach * stretch + token, s, -jnp.inf)
        s_scr[at, :] = s
        dp_scr[at, :] = dp
        peak = jnp.max(jnp.maximum(peak, fold(s, jnp.max)), axis=0, keepdims=True)

        def sums(t, carry):
            total, delta = carry
            at = pl.ds(pl.multiple_of(t * TILE, TILE), TILE)
            e = jnp.exp2(s_scr[at, :] - peak)
            s_scr[at, :] = e
            return total + fold(e, jnp.sum), delta + fold(e * dp_scr[at, :], jnp.sum)

        zero = jnp.zeros((8, TILE), F32)
        total, delta = lax.fori_loop(0, last + 1, sums, (zero, zero))
        inverse = 1.0 / jnp.sum(total, axis=0, keepdims=True)
        delta = jnp.sum(delta, axis=0, keepdims=True) * inverse

        def grads(t, dqt):
            at = pl.ds(pl.multiple_of(t * TILE, TILE), TILE)
            p = s_scr[at, :] * inverse
            ds = p * (dp_scr[at, :] - delta)
            dv_acc[at, :] += dot(jnp.concatenate(split2(p), axis=1), do_rhs)
            h, l = split2(ds)
            dk_acc[at, :] += dot(jnp.concatenate([h, l], axis=1), q_rhs)
            return dqt + dot(ktrans[t], h) + dot(ktrans[t], l)

        dqt = lax.fori_loop(0, last + 1, grads, jnp.zeros((2 * HEAD_SIZE, TILE), F32))
        dq = ((dqt[:HEAD_SIZE] + dqt[HEAD_SIZE:]) * SCORE_SCALE).T
        for g in range(GROUP_LIST):
            dq_ref[0, rows, g * HEAD_SIZE : (g + 1) * HEAD_SIZE] = dq[g * stretch : (g + 1) * stretch]

    @pl.when(step == pl.num_programs(0) - 1)
    def _():
        for j in range(blocks):
            ref, at = (down_ref, j) if j < inner_count else (dprev_ref, j - inner_count)
            for half in range(2):
                slot = jnp.where(low_half[j] == half, rank[j], 2 * blocks - 1 - rank[j])
                came = pl.ds(pl.multiple_of(slot * stretch, stretch), stretch)
                to = slice(half * stretch, (half + 1) * stretch)
                dk, dv = dk_acc[came, :], dv_acc[came, :]
                ref[at, to, :HEAD_SIZE] = (dk[:, :HEAD_SIZE] + dk[:, HEAD_SIZE:]) * (1.0 / LOG2E)
                ref[at, to, HEAD_SIZE:] = dv[:, :HEAD_SIZE] + dv[:, HEAD_SIZE:]


def attention(inner_count, outer_count, seg, q, do, own, prev):
    rows = own.shape[1]
    keys = 2 * inner_count * rows
    block = lambda width: pl.BlockSpec((1, rows, width), lambda i: (i, 0, 0))
    whole = pl.BlockSpec((inner_count, rows, 2 * HEAD_SIZE), lambda i: (0, 0, 0))
    kv_shape = jax.ShapeDtypeStruct(own.shape, F32)
    return pl.pallas_call(
        functools.partial(attention_kernel, inner_count, outer_count),
        grid=(inner_count,),
        in_specs=[
            pl.BlockSpec(memory_space=pltpu.SMEM),
            block(HEAD_WIDTH), block(HEAD_WIDTH), whole, whole,
        ],
        out_specs=[block(HEAD_WIDTH), whole, whole],
        out_shape=[jax.ShapeDtypeStruct((inner_count, rows, HEAD_WIDTH), F32), kv_shape, kv_shape],
        scratch_shapes=[
            pltpu.SMEM((2 * inner_count,), jnp.int32),
            pltpu.SMEM((2 * inner_count,), jnp.int32),
            pltpu.VMEM((keys, HEAD_SIZE), F32),
            pltpu.VMEM((keys, 6 * HEAD_SIZE), BF16),
            pltpu.VMEM((keys, 4 * HEAD_SIZE), BF16),
            pltpu.VMEM((keys // TILE, 2 * HEAD_SIZE, TILE), BF16),
            pltpu.VMEM((keys, 2 * HEAD_SIZE), F32),
            pltpu.VMEM((keys, 2 * HEAD_SIZE), F32),
            pltpu.VMEM((keys, TILE), F32),
            pltpu.VMEM((keys, TILE), F32),
        ],
        compiler_params=pltpu.CompilerParams(vmem_limit_bytes=48 * 1024 * 1024),
        name="attention",
    )(seg, q, do, own, prev)


def from_behind(x, axis, by):
    size = lax.axis_size(axis)
    return lax.ppermute(x, axis, [(i, (i + by) % size) for i in range(size)])


def by_head(x, heads):
    rows = x.shape[0]
    return x.reshape(rows, heads, -1).transpose(1, 0, 2)


def local(query, keys, values, grad_out, segment_number):
    inner_count = lax.axis_size("inner")
    outer_count = lax.axis_size("outer")
    rows = query.shape[0]
    swap = lambda x: lax.all_to_all(x, "inner", 0, 0)
    own = swap(jnp.concatenate([by_head(keys, inner_count), by_head(values, inner_count)], axis=2))
    prev = from_behind(own, "outer", 1)
    both = swap(jnp.stack([by_head(query, inner_count), by_head(grad_out, inner_count)], axis=1))
    q, do = both[:, 0], both[:, 1]
    dq, down, dprev = attention(inner_count, outer_count, segment_number.T, q, do, own, prev)
    back = from_behind(dprev, "outer", -1)
    dq = swap(dq).transpose(1, 0, 2).reshape(rows, -1)
    dkv = swap(down + back).transpose(1, 0, 2)
    return (
        dq,
        dkv[:, :, :HEAD_SIZE].reshape(rows, -1),
        dkv[:, :, HEAD_SIZE:].reshape(rows, -1),
    )


def solution(mesh):
    spec = P(("inner", "outer"), None)
    return jax.shard_map(
        local,
        mesh=mesh,
        in_specs=(spec, spec, spec, spec, P()),
        out_specs=(spec, spec, spec),
        check_vma=False,
    )
```

time: 788 us -> 230 us (0.29)
  waiting for transfers between devices: 462 us -> 103 us
  matrix products: 239 us -> 0 us
  Pallas kernels: 0 us -> 65.4 us
  other arithmetic: 32.1 us -> 6.16 us
  starting transfers between devices: 8.99 us -> 30 us
  between operations: 13.9 us -> 0.74 us
    dot_general x40 -> x0, matrix products: 239 us -> none  [the longest x8 64.9 us: head_stride(): jnp.einsum('gtl,tgd->ld', score_grads, query_head, precision=lax.Precisio...]
    all_gather x2 -> x0, waiting for transfers between devices: 181 us -> none  [the longest x1 105 us: local(): lax.all_gather(keys, 'inner', axis=0, tiled=True)]
    reduce_scatter x2 -> x0, waiting for transfers between devices: 134 us -> none  [the longest x1 88.2 us: local(): lax.psum_scatter(payload_partial_contributions[:local_interval] + returni...]
    ppermute x4 -> x2, waiting for transfers between devices: 145 us -> 46.4 us  [from_behind(): return lax.ppermute(x, axis, [(i, (i + by) % size) for i in range(size)])]
    pallas_call x0 -> x1, Pallas kernels: none -> 65.4 us  [attention(): pl.pallas_call(functools.partial(attention_kernel, inner_count, outer_cou...]
    all_to_all x0 -> x4, waiting for transfers between devices: none -> 56.8 us  [local(): swap = lambda x: lax.all_to_all(x, 'inner', 0, 0)]
    all_to_all x0 -> x4, starting transfers between devices: none -> 27.5 us  [local(): swap = lambda x: lax.all_to_all(x, 'inner', 0, 0)]
    concatenate x3 -> x1, other arithmetic: 15.3 us -> 1.13 us  [local(): jnp.concatenate([by_head(keys, inner_count), by_head(values, inner_count)...]
  transfers between devices with their start and end apart: 8 -> 6, of which waited for: 7 -> 5; matrix products, arithmetic and copies ran while one was open for 3% -> 10% of each run, Pallas kernels for 0% -> 0%
where the time goes in v1:
time: 230 us
  waiting for transfers between devices  103 us (45%)
  Pallas kernels  65.4 us (28%)
  starting transfers between devices  30 us (13%)
  local copies, waits for them, and re-layouts  24.1 us (10%)
  other arithmetic  6.16 us (3%)
    pallas_call x1, Pallas kernels, attention(): pl.pallas_call(functools.partial(attention_kernel, inner_count, outer_cou...  65.4 us
    all_to_all x4, waiting for transfers between devices, local(): swap = lambda x: lax.all_to_all(x, 'inner', 0, 0)  56.8 us
    ppermute x2, waiting for transfers between devices, from_behind(): return lax.ppermute(x, axis, [(i, (i + by) % size) for i in range(size)])  46.4 us
    all_to_all x4, starting transfers between devices, local(): swap = lambda x: lax.all_to_all(x, 'inner', 0, 0)  27.5 us
    unnamed x15, local copies, waits for them, and re-layouts  11.1 us
    another operation x1, local copies, waits for them, and re-layouts, local(): jnp.stack([by_head(query, inner_count), by_head(grad_out, inner_count)],...  5.39 us
    squeeze x1, local copies, waits for them, and re-layouts, local(): q, do = (both[:, 0], both[:, 1])  4.85 us
  transfers between devices with their start and end apart: 6, of which 5 were waited for; matrix products, arithmetic and copies ran while one was open for 10% of the time, Pallas kernels for 0%

profile of v1, /device:TPU:1, one launch (start us, length us, event | category | flops | bytes accessed | tf_op | source)
XLA Modules:
  0.0 229.6 jit_solution(6239534599735060946)
XLA Ops:
  0.6 0.0 copy-start.3
  0.6 1.3 copy.27
  1.9 0.2 copy.28
  2.1 0.0 copy-done.3
  2.2 0.2 copy.29
  2.4 0.2 copy.30
  2.6 1.1 pad_maximum_fusion.1
  3.7 8.5 %all-to-all-start.1 = ((f32[8,128,256]{2,1,0:T(8,128)}), f32[8,128,256]{2,1,0:T(8,128)S(1)}, u32[]{:S(2)}, u32[]{:S(2)}) async-start(f32[8,128,256]{2,1,0:T(8,128)} %pad_maximum_fusion.1), calls=%async_computation.1 | async-start | bytes 2097152 | tf_op jit(solution)/shard_map/all_to_all | solution.py:218
  12.2 1.9 copy.22
  14.1 2.9 %copy.23 = f32[128,4096]{0,1:T(8,128)} copy(f32[128,4096]{1,0:T(8,128)} %param.8) | data formatting | bytes 4194304 | tf_op args[3]
  17.0 3.9 %pad_maximum_fusion = f32[8,2,128,512]{2,3,0,1:T(8,128)} fusion(f32[8,1,128,512]{2,3,0,1:T(8,128)} %bitcast.31, f32[8,1,128,512]{2,3,0,1:T(8,128)S(1)} %bitcast.30), kind=kLoop, calls=%fused_computation | loop fusion | flops 1048576 | bytes 8388608 | tf_op jit(solution)/shard_map/stack | solution.py:221
  20.9 5.4 %copy.24 = f32[8,2,128,512]{3,2,1,0:T(8,128)} copy(f32[8,2,128,512]{2,3,0,1:T(8,128)} %pad_maximum_fusion) | data formatting | bytes 8388608 | tf_op jit(solution)/shard_map/stack | solution.py:221
  26.2 1.9 all-to-all-done.1.own_ref
  28.2 4.7 %all-to-all-start = ((f32[8,2,128,512]{3,2,1,0:T(8,128)}), f32[8,2,128,512]{3,2,1,0:T(8,128)}, u32[]{:S(2)}, u32[]{:S(2)}) async-start(f32[8,2,128,512]{3,2,1,0:T(8,128)} %copy.24), calls=%async_computation | async-start | bytes 8388608 | tf_op jit(solution)/shard_map/all_to_all | solution.py:218
  32.9 0.0 copy-start
  32.9 2.4 %collective-permute-start = (f32[8,128,256]{2,1,0:T(8,128)S(1)}, f32[8,128,256]{2,1,0:T(8,128)S(1)}, u32[]{:S(2)}, u32[]{:S(2)}) collective-permute-start(f32[8,128,256]{2,1,0:T(8,128)S(1)} %all-to-all-done.1.own_ref), channel_id=1, source_target_pairs={{0,1},{1,2},{2,3},{3,4},{4,5},{5,6},{6,7},{7,8},{8,9},{9,10},{10,1... | collective-permute-start | bytes 3145736 | tf_op jit(solution)/shard_map/ppermute | solution.py:206
  35.3 46.7 %all-to-all-done = f32[8,2,128,512]{3,2,1,0:T(8,128)} async-done(((f32[8,2,128,512]{3,2,1,0:T(8,128)}), f32[8,2,128,512]{3,2,1,0:T(8,128)}, u32[]{:S(2)}, u32[]{:S(2)}) %all-to-all-start) | async-done | bytes 4194336 | tf_op jit(solution)/shard_map/all_to_all | solution.py:218
  82.0 4.8 %slice_bitcast_fusion = (f32[8,128,512]{2,1,0:T(8,128)}, f32[8,128,512]{2,1,0:T(8,128)}) fusion(f32[8,2,128,512]{3,2,1,0:T(8,128)} %all-to-all-done), kind=kLoop, calls=%fused_computation.1 | loop fusion | bytes 8388608 | tf_op jit(solution)/shard_map/squeeze | solution.py:222
  86.9 3.2 %collective-permute-done.prev_ref = f32[8,128,256]{2,1,0:T(8,128)S(1)} collective-permute-done((f32[8,128,256]{2,1,0:T(8,128)S(1)}, f32[8,128,256]{2,1,0:T(8,128)S(1)}, u32[]{:S(2)}, u32[]{:S(2)}) %collective-permute-start) | collective-permute-done | bytes 1048608 | tf_op jit(solution)/shard_map/ppermute | solution.py:206
  90.0 0.0 copy-done
  90.0 65.4 %attention.1 = (f32[8,128,512]{2,1,0:T(8,128)}, f32[8,128,256]{2,1,0:T(8,128)S(1)}, f32[8,128,256]{2,1,0:T(8,128)S(1)}) custom-call(s32[2,128]{1,0:T(2,128)S(1)} %bitcast.28, f32[8,128,512]{2,1,0:T(8,128)} %get-tuple-element.16.q_ref, f32[8,128,512]{2,1,0:T(8,128)} %get-tuple-element.15.do_ref, f32[8,128,256]{2,1,0:T(8,128)S(1)} %all-to-all-done.1.own_ref, ...), custom_call_target="tpu_custom_call" | custom-call | tf_op jit(solution)/shard_map/attention/pallas_call | solution.py:178
  155.5 0.0 copy-start.1
  155.5 1.0 copy-done.1
  156.4 0.0 copy-start.2
  156.4 7.1 %all-to-all-start.2 = ((f32[8,128,512]{2,1,0:T(8,128)}), f32[8,128,512]{2,1,0:T(8,128)}, u32[]{:S(2)}, u32[]{:S(2)}) async-start(f32[8,128,512]{2,1,0:T(8,128)} %get-tuple-element.6), calls=%async_computation.2 | async-start | bytes 4194304 | tf_op jit(solution)/shard_map/all_to_all | solution.py:218
  163.6 0.0 copy-done.2
  163.6 0.1 collective-permute-start.1
  163.6 43.3 %collective-permute-done.1 = f32[8,128,256]{2,1,0:T(8,128)S(1)} collective-permute-done((f32[8,128,256]{2,1,0:T(8,128)S(1)}, f32[8,128,256]{2,1,0:T(8,128)S(1)}, u32[]{:S(2)}, u32[]{:S(2)}) %collective-permute-start.1) | collective-permute-done | bytes 1048608 | tf_op jit(solution)/shard_map/ppermute | solution.py:206
  206.9 1.2 add.3
  208.1 0.0 all-to-all-done.2
  208.1 7.2 %all-to-all-start.3 = ((f32[8,128,256]{2,1,0:T(8,128)}), f32[8,128,256]{2,1,0:T(8,128)S(1)}, u32[]{:S(2)}, u32[]{:S(2)}) async-start(f32[8,128,256]{2,1,0:T(8,128)} %add.3), calls=%async_computation.3 | async-start | bytes 2097152 | tf_op jit(solution)/shard_map/all_to_all | solution.py:218
  215.3 1.9 copy.31
  217.2 1.8 copy.34
  219.0 8.1 %all-to-all-done.3 = f32[8,128,256]{2,1,0:T(8,128)S(1)} async-done(((f32[8,128,256]{2,1,0:T(8,128)}), f32[8,128,256]{2,1,0:T(8,128)S(1)}, u32[]{:S(2)}, u32[]{:S(2)}) %all-to-all-start.3) | async-done | bytes 1048608 | tf_op jit(solution)/shard_map/all_to_all | solution.py:218
  227.1 0.1 fusion
  227.2 0.2 copy.32
  227.4 1.0 copy.35
  228.4 0.2 copy.33
  228.6 1.0 copy.36
Async XLA Ops:
  0.6 1.5 copy-start.3
  3.7 24.5 %all-to-all-start.1 = ((f32[8,128,256]{2,1,0:T(8,128)}), f32[8,128,256]{2,1,0:T(8,128)S(1)}, u32[]{:S(2)}, u32[]{:S(2)}) async-start(f32[8,128,256]{2,1,0:T(8,128)} %pad_maximum_fusion.1), calls=%async_computation.1 | async-start | bytes 2097152 | tf_op jit(solution)/shard_map/all_to_all | solution.py:218
  28.2 53.8 %all-to-all-start = ((f32[8,2,128,512]{3,2,1,0:T(8,128)}), f32[8,2,128,512]{3,2,1,0:T(8,128)}, u32[]{:S(2)}, u32[]{:S(2)}) async-start(f32[8,2,128,512]{3,2,1,0:T(8,128)} %copy.24), calls=%async_computation | async-start | bytes 8388608 | tf_op jit(solution)/shard_map/all_to_all | solution.py:218
  32.9 57.1 %copy-start = (s32[128,2]{0,1:T(2,128)S(1)}, s32[128,2]{0,1:T(2,128)}, u32[]{:S(2)}) copy-start(s32[128,2]{0,1:T(2,128)} %param.9) | copy-start | bytes 3076
  32.9 57.1 %collective-permute-start = (f32[8,128,256]{2,1,0:T(8,128)S(1)}, f32[8,128,256]{2,1,0:T(8,128)S(1)}, u32[]{:S(2)}, u32[]{:S(2)}) collective-permute-start(f32[8,128,256]{2,1,0:T(8,128)S(1)} %all-to-all-done.1.own_ref), channel_id=1, source_target_pairs={{0,1},{1,2},{2,3},{3,4},{4,5},{5,6},{6,7},{7,8},{8,9},{9,10},{10,1... | collective-permute-start | bytes 3145736 | tf_op jit(solution)/shard_map/ppermute | solution.py:206
  155.5 1.0 copy-start.1
  156.4 7.1 %copy-start.2 = (f32[8,128,256]{2,1,0:T(8,128)S(1)}, f32[8,128,256]{2,1,0:T(8,128)}, u32[]{:S(2)}) copy-start(f32[8,128,256]{2,1,0:T(8,128)} %copy-done.1) | copy-start | bytes 3145732
  156.4 51.6 %all-to-all-start.2 = ((f32[8,128,512]{2,1,0:T(8,128)}), f32[8,128,512]{2,1,0:T(8,128)}, u32[]{:S(2)}, u32[]{:S(2)}) async-start(f32[8,128,512]{2,1,0:T(8,128)} %get-tuple-element.6), calls=%async_computation.2 | async-start | bytes 4194304 | tf_op jit(solution)/shard_map/all_to_all | solution.py:218
  163.6 43.3 %collective-permute-start.1 = (f32[8,128,256]{2,1,0:T(8,128)S(1)}, f32[8,128,256]{2,1,0:T(8,128)S(1)}, u32[]{:S(2)}, u32[]{:S(2)}) collective-permute-start(f32[8,128,256]{2,1,0:T(8,128)S(1)} %copy-done.2), channel_id=1, source_target_pairs={{0,15},{1,0},{2,1},{3,2},{4,3},{5,4},{6,5},{7,6},{8,7},{9,8},{10,9... | collective-permute-start | bytes 3145736 | tf_op jit(solution)/shard_map/ppermute | solution.py:206
  208.1 19.1 %all-to-all-start.3 = ((f32[8,128,256]{2,1,0:T(8,128)}), f32[8,128,256]{2,1,0:T(8,128)S(1)}, u32[]{:S(2)}, u32[]{:S(2)}) async-start(f32[8,128,256]{2,1,0:T(8,128)} %add.3), calls=%async_computation.3 | async-start | bytes 2097152 | tf_op jit(solution)/shard_map/all_to_all | solution.py:218
